TPU v7x, 256 devices: a whole 4x4x8 slice. The times are simulated.
256 devices in a mesh: layer: 32 (over z, x), iface: 8 (over y, core).
Axes of the slice: x: 4, y: 4, z: 8, core: 2. Of those that a mesh axis runs over, the one named last changes fastest.
Arguments:
- green_down: bfloat16 [32, 2, 2048, 2048], P('layer', None, 'iface'), may hold values from -0.09375 to 0.09375
- green_up: bfloat16 [32, 2, 2048, 2048], P('layer', None, 'iface'), may hold values from -0.09375 to 0.09375
- source_down: bfloat16 [32, 2, 96, 2048], P('layer', None, None, 'iface'), may hold values from -2 to 2
- source_up: bfloat16 [32, 2, 96, 2048], P('layer', None, None, 'iface'), may hold values from -2 to 2
Outputs:
- down_traces: bfloat16 [32, 2, 96, 2048], P('layer', None, None, 'iface')
- up_traces: bfloat16 [32, 2, 96, 2048], P('layer', None, None, 'iface')
All inputs are finite; a program needn't handle non-finite values.
Results may differ from a plain program's by a relative error of at most 0.027.
Values may be sent and summed in bfloat16 or wider, within the bound.
A program may use at most 64 MiB of HBM per device.

v0:
```python
import jax
import jax.numpy as jnp
from jax import lax
from jax.sharding import PartitionSpec as P

BATCHES = 8


def shifted(block, axis, distance):
    devices = range(lax.axis_size(axis))
    route = [(i - distance, i) for i in devices if i - distance in devices]
    return lax.ppermute(block, axis, route)


def complex_apply(matrix, traces):
    products = lax.dot_general(
        traces, matrix, (((2,), (2,)), ((), ())), preferred_element_type=jnp.float32
    )
    real_part = products[0, :, 0] - products[1, :, 1]
    imag_part = products[0, :, 1] + products[1, :, 0]
    return jnp.stack([real_part, imag_part])


def advance(position, step_no, batch_count, batch_width, source, outputs, incoming, matrix):
    batch_idx = step_no - position
    is_valid = jnp.logical_and(batch_idx >= 0, batch_idx < batch_count)
    first_row = jnp.clip(batch_idx, 0, batch_count - 1) * batch_width
    src_part = lax.dynamic_slice_in_dim(source, first_row, batch_width, 1)
    fresh = (complex_apply(matrix, incoming) + src_part.astype(jnp.float32)).astype(jnp.bfloat16)
    previous = lax.dynamic_slice_in_dim(outputs, first_row, batch_width, 1)
    outputs = lax.dynamic_update_slice_in_dim(
        outputs, jnp.where(is_valid, fresh, previous), first_row, 1
    )
    return (fresh, outputs)


def on_device(green_down, green_up, source_down, source_up):
    local_down = green_down[0]
    local_up = green_up[0]
    src_down = source_down[0]
    src_up = source_up[0]
    layer_count = lax.axis_size("layer")
    position = lax.axis_index("layer")
    shot_count = src_down.shape[1]
    piece_rows = src_down.shape[2]
    batch_count = BATCHES
    batch_width = shot_count // batch_count
    step_count = layer_count + batch_count - 1
    reversed_pos = layer_count - 1 - position
    empty_out = jnp.zeros((2, shot_count, piece_rows), jnp.bfloat16)

    def loop_body(step_no, state):
        piece_down, piece_up, out_down, out_up = state
        full_down, full_up = (
            lax.all_gather(piece_down, "iface", axis=2, tiled=True),
            lax.all_gather(piece_up, "iface", axis=2, tiled=True),
        )
        fresh_down, out_down = advance(
            position, step_no, batch_count, batch_width, src_down, out_down, full_down, local_down
        )
        fresh_up, out_up = advance(
            reversed_pos, step_no, batch_count, batch_width, src_up, out_up, full_up, local_up
        )
        piece_down = shifted(fresh_down, "layer", 1)
        piece_up = shifted(fresh_up, "layer", -1)
        return (piece_down, piece_up, out_down, out_up)

    zero_piece = jnp.zeros((2, batch_width, piece_rows), jnp.bfloat16)
    state = lax.fori_loop(0, step_count, loop_body, (zero_piece, zero_piece, empty_out, empty_out))
    return (state[2][None], state[3][None])


def solution(mesh):
    in_specs = (
        P("layer", None, "iface", None),
        P("layer", None, "iface", None),
        P("layer", None, None, "iface"),
        P("layer", None, None, "iface"),
    )
    out_specs = (P("layer", None, None, "iface"), P("layer", None, None, "iface"))
    return jax.shard_map(
        on_device, mesh=mesh, in_specs=in_specs, out_specs=out_specs, check_vma=False
    )
```

profile of v0, /device:TPU:128, one launch (start us, length us, event | category | flops | bytes accessed | tf_op | source)
XLA Modules:
  0.0 1610.9 jit_solution(12180050433712579687)
XLA Ops:
  0.7 1609.5 %while.19 = (s32[]{:T(128)}, bf16[2,12,256]{2,1,0:T(8,128)(2,1)S(1)}, bf16[2,12,256]{2,1,0:T(8,128)(2,1)S(1)}, bf16[2,96,256]{2,1,0:T(8,128)(2,1)S(1)}, bf16[2,9...) while((s32[]{:T(128)}, ...), condition=%wide.region_1.2_spmd, body=%wide.region_0.1_spmd.sunk | while | flops 100737040 | bytes 13541865 | solution.py:69
  0.7 13.4 all_gather.17
  21.5 12.8 all_gather.16
  44.8 12.9 all_gather.17
  62.7 12.8 all_gather.16
  86.0 12.9 all_gather.17
  103.9 12.8 all_gather.16
  127.2 12.9 all_gather.17
  145.1 12.8 all_gather.16
  168.4 12.9 all_gather.17
  186.4 12.8 all_gather.16
  209.6 12.9 all_gather.17
  227.6 12.8 all_gather.16
  250.8 12.9 all_gather.17
  268.8 12.8 all_gather.16
  292.0 12.9 all_gather.17
  310.0 12.8 all_gather.16
  333.3 12.9 all_gather.17
  351.2 12.8 all_gather.16
  374.5 12.9 all_gather.17
  392.4 12.8 all_gather.16
  415.7 12.9 all_gather.17
  433.6 12.8 all_gather.16
  456.9 12.9 all_gather.17
  474.9 12.8 all_gather.16
  498.1 12.9 all_gather.17
  516.1 12.8 all_gather.16
  539.3 12.9 all_gather.17
  557.3 12.8 all_gather.16
  580.5 12.9 all_gather.17
  598.5 12.8 all_gather.16
  621.8 12.9 all_gather.17
  639.7 12.8 all_gather.16
  663.0 12.9 all_gather.17
  680.9 12.8 all_gather.16
  704.2 12.9 all_gather.17
  722.1 12.8 all_gather.16
  745.4 12.9 all_gather.17
  763.3 12.8 all_gather.16
  786.6 12.9 all_gather.17
  804.6 12.8 all_gather.16
  827.8 12.9 all_gather.17
  869.0 12.9 all_gather.17
  887.0 12.8 all_gather.16
  910.2 12.9 all_gather.17
  951.4 12.9 all_gather.17
  969.4 12.8 all_gather.16
  992.6 12.9 all_gather.17
  1033.8 12.9 all_gather.17
  1075.0 12.9 all_gather.17
  1116.1 12.9 all_gather.17
  1157.3 12.9 all_gather.17
  1198.5 12.9 all_gather.17
  1239.7 12.9 all_gather.17
  1280.8 12.9 all_gather.17
  1298.8 12.8 all_gather.16
  1322.0 12.9 all_gather.17
  1363.2 12.9 all_gather.17
  1404.3 12.9 all_gather.17
  1422.3 12.8 all_gather.16
  1445.5 12.9 all_gather.17
  1486.7 12.9 all_gather.17
  1527.9 12.9 all_gather.17
  1569.0 12.9 all_gather.17
  (569 shorter events, 796.5 us)
Async XLA Ops:
  17.3 20.9 %collective-permute-start.1 = (bf16[2,12,256]{2,1,0:T(8,128)(2,1)S(1)}, bf16[2,12,256]{2,1,0:T(8,128)(2,1)S(1)}, u32[]{:S(2)}, u32[]{:S(2)}) collective-permute-start(bf16[2,12,256]{2,1,0:T(8,128)(2,1)S(1)} %get-tuple-element.299), channel_id=1, source_target_pairs={{8,0},{16,8},{24,16},{32,24},{40,32},{48,40},{56,48},{64,56},{72,6... | collective-permute-start | bytes 36872 | tf_op jit(solution)/shard_map/while/body/eval_jaxpr/ppermute | solution.py:12
  35.8 9.0 collective-permute-start
  60.8 20.6 %collective-permute-start.1 = (bf16[2,12,256]{2,1,0:T(8,128)(2,1)S(1)}, bf16[2,12,256]{2,1,0:T(8,128)(2,1)S(1)}, u32[]{:S(2)}, u32[]{:S(2)}) collective-permute-start(bf16[2,12,256]{2,1,0:T(8,128)(2,1)S(1)} %get-tuple-element.299), channel_id=1, source_target_pairs={{8,0},{16,8},{24,16},{32,24},{40,32},{48,40},{56,48},{64,56},{72,6... | collective-permute-start | bytes 36872 | tf_op jit(solution)/shard_map/while/body/eval_jaxpr/ppermute | solution.py:12
  77.0 9.0 collective-permute-start
  102.0 20.6 %collective-permute-start.1 = (bf16[2,12,256]{2,1,0:T(8,128)(2,1)S(1)}, bf16[2,12,256]{2,1,0:T(8,128)(2,1)S(1)}, u32[]{:S(2)}, u32[]{:S(2)}) collective-permute-start(bf16[2,12,256]{2,1,0:T(8,128)(2,1)S(1)} %get-tuple-element.299), channel_id=1, source_target_pairs={{8,0},{16,8},{24,16},{32,24},{40,32},{48,40},{56,48},{64,56},{72,6... | collective-permute-start | bytes 36872 | tf_op jit(solution)/shard_map/while/body/eval_jaxpr/ppermute | solution.py:12
  118.2 9.0 collective-permute-start
  143.2 20.6 %collective-permute-start.1 = (bf16[2,12,256]{2,1,0:T(8,128)(2,1)S(1)}, bf16[2,12,256]{2,1,0:T(8,128)(2,1)S(1)}, u32[]{:S(2)}, u32[]{:S(2)}) collective-permute-start(bf16[2,12,256]{2,1,0:T(8,128)(2,1)S(1)} %get-tuple-element.299), channel_id=1, source_target_pairs={{8,0},{16,8},{24,16},{32,24},{40,32},{48,40},{56,48},{64,56},{72,6... | collective-permute-start | bytes 36872 | tf_op jit(solution)/shard_map/while/body/eval_jaxpr/ppermute | solution.py:12
  159.5 9.0 collective-permute-start
  184.4 20.6 %collective-permute-start.1 = (bf16[2,12,256]{2,1,0:T(8,128)(2,1)S(1)}, bf16[2,12,256]{2,1,0:T(8,128)(2,1)S(1)}, u32[]{:S(2)}, u32[]{:S(2)}) collective-permute-start(bf16[2,12,256]{2,1,0:T(8,128)(2,1)S(1)} %get-tuple-element.299), channel_id=1, source_target_pairs={{8,0},{16,8},{24,16},{32,24},{40,32},{48,40},{56,48},{64,56},{72,6... | collective-permute-start | bytes 36872 | tf_op jit(solution)/shard_map/while/body/eval_jaxpr/ppermute | solution.py:12
  200.7 9.0 collective-permute-start
  225.6 20.6 %collective-permute-start.1 = (bf16[2,12,256]{2,1,0:T(8,128)(2,1)S(1)}, bf16[2,12,256]{2,1,0:T(8,128)(2,1)S(1)}, u32[]{:S(2)}, u32[]{:S(2)}) collective-permute-start(bf16[2,12,256]{2,1,0:T(8,128)(2,1)S(1)} %get-tuple-element.299), channel_id=1, source_target_pairs={{8,0},{16,8},{24,16},{32,24},{40,32},{48,40},{56,48},{64,56},{72,6... | collective-permute-start | bytes 36872 | tf_op jit(solution)/shard_map/while/body/eval_jaxpr/ppermute | solution.py:12
  241.9 9.0 collective-permute-start
  266.8 20.6 %collective-permute-start.1 = (bf16[2,12,256]{2,1,0:T(8,128)(2,1)S(1)}, bf16[2,12,256]{2,1,0:T(8,128)(2,1)S(1)}, u32[]{:S(2)}, u32[]{:S(2)}) collective-permute-start(bf16[2,12,256]{2,1,0:T(8,128)(2,1)S(1)} %get-tuple-element.299), channel_id=1, source_target_pairs={{8,0},{16,8},{24,16},{32,24},{40,32},{48,40},{56,48},{64,56},{72,6... | collective-permute-start | bytes 36872 | tf_op jit(solution)/shard_map/while/body/eval_jaxpr/ppermute | solution.py:12
  283.1 9.0 collective-permute-start
  308.1 20.6 %collective-permute-start.1 = (bf16[2,12,256]{2,1,0:T(8,128)(2,1)S(1)}, bf16[2,12,256]{2,1,0:T(8,128)(2,1)S(1)}, u32[]{:S(2)}, u32[]{:S(2)}) collective-permute-start(bf16[2,12,256]{2,1,0:T(8,128)(2,1)S(1)} %get-tuple-element.299), channel_id=1, source_target_pairs={{8,0},{16,8},{24,16},{32,24},{40,32},{48,40},{56,48},{64,56},{72,6... | collective-permute-start | bytes 36872 | tf_op jit(solution)/shard_map/while/body/eval_jaxpr/ppermute | solution.py:12
  324.3 9.0 collective-permute-start
  349.3 20.6 %collective-permute-start.1 = (bf16[2,12,256]{2,1,0:T(8,128)(2,1)S(1)}, bf16[2,12,256]{2,1,0:T(8,128)(2,1)S(1)}, u32[]{:S(2)}, u32[]{:S(2)}) collective-permute-start(bf16[2,12,256]{2,1,0:T(8,128)(2,1)S(1)} %get-tuple-element.299), channel_id=1, source_target_pairs={{8,0},{16,8},{24,16},{32,24},{40,32},{48,40},{56,48},{64,56},{72,6... | collective-permute-start | bytes 36872 | tf_op jit(solution)/shard_map/while/body/eval_jaxpr/ppermute | solution.py:12
  365.5 9.0 collective-permute-start
  390.5 20.6 %collective-permute-start.1 = (bf16[2,12,256]{2,1,0:T(8,128)(2,1)S(1)}, bf16[2,12,256]{2,1,0:T(8,128)(2,1)S(1)}, u32[]{:S(2)}, u32[]{:S(2)}) collective-permute-start(bf16[2,12,256]{2,1,0:T(8,128)(2,1)S(1)} %get-tuple-element.299), channel_id=1, source_target_pairs={{8,0},{16,8},{24,16},{32,24},{40,32},{48,40},{56,48},{64,56},{72,6... | collective-permute-start | bytes 36872 | tf_op jit(solution)/shard_map/while/body/eval_jaxpr/ppermute | solution.py:12
  406.7 9.0 collective-permute-start
  431.7 20.6 %collective-permute-start.1 = (bf16[2,12,256]{2,1,0:T(8,128)(2,1)S(1)}, bf16[2,12,256]{2,1,0:T(8,128)(2,1)S(1)}, u32[]{:S(2)}, u32[]{:S(2)}) collective-permute-start(bf16[2,12,256]{2,1,0:T(8,128)(2,1)S(1)} %get-tuple-element.299), channel_id=1, source_target_pairs={{8,0},{16,8},{24,16},{32,24},{40,32},{48,40},{56,48},{64,56},{72,6... | collective-permute-start | bytes 36872 | tf_op jit(solution)/shard_map/while/body/eval_jaxpr/ppermute | solution.py:12
  447.9 9.0 collective-permute-start
  472.9 20.6 %collective-permute-start.1 = (bf16[2,12,256]{2,1,0:T(8,128)(2,1)S(1)}, bf16[2,12,256]{2,1,0:T(8,128)(2,1)S(1)}, u32[]{:S(2)}, u32[]{:S(2)}) collective-permute-start(bf16[2,12,256]{2,1,0:T(8,128)(2,1)S(1)} %get-tuple-element.299), channel_id=1, source_target_pairs={{8,0},{16,8},{24,16},{32,24},{40,32},{48,40},{56,48},{64,56},{72,6... | collective-permute-start | bytes 36872 | tf_op jit(solution)/shard_map/while/body/eval_jaxpr/ppermute | solution.py:12
  514.1 20.6 %collective-permute-start.1 = (bf16[2,12,256]{2,1,0:T(8,128)(2,1)S(1)}, bf16[2,12,256]{2,1,0:T(8,128)(2,1)S(1)}, u32[]{:S(2)}, u32[]{:S(2)}) collective-permute-start(bf16[2,12,256]{2,1,0:T(8,128)(2,1)S(1)} %get-tuple-element.299), channel_id=1, source_target_pairs={{8,0},{16,8},{24,16},{32,24},{40,32},{48,40},{56,48},{64,56},{72,6... | collective-permute-start | bytes 36872 | tf_op jit(solution)/shard_map/while/body/eval_jaxpr/ppermute | solution.py:12
  530.4 9.0 collective-permute-start
  555.3 20.6 %collective-permute-start.1 = (bf16[2,12,256]{2,1,0:T(8,128)(2,1)S(1)}, bf16[2,12,256]{2,1,0:T(8,128)(2,1)S(1)}, u32[]{:S(2)}, u32[]{:S(2)}) collective-permute-start(bf16[2,12,256]{2,1,0:T(8,128)(2,1)S(1)} %get-tuple-element.299), channel_id=1, source_target_pairs={{8,0},{16,8},{24,16},{32,24},{40,32},{48,40},{56,48},{64,56},{72,6... | collective-permute-start | bytes 36872 | tf_op jit(solution)/shard_map/while/body/eval_jaxpr/ppermute | solution.py:12
  596.5 20.6 %collective-permute-start.1 = (bf16[2,12,256]{2,1,0:T(8,128)(2,1)S(1)}, bf16[2,12,256]{2,1,0:T(8,128)(2,1)S(1)}, u32[]{:S(2)}, u32[]{:S(2)}) collective-permute-start(bf16[2,12,256]{2,1,0:T(8,128)(2,1)S(1)} %get-tuple-element.299), channel_id=1, source_target_pairs={{8,0},{16,8},{24,16},{32,24},{40,32},{48,40},{56,48},{64,56},{72,6... | collective-permute-start | bytes 36872 | tf_op jit(solution)/shard_map/while/body/eval_jaxpr/ppermute | solution.py:12
  612.8 9.0 collective-permute-start
  637.8 20.6 %collective-permute-start.1 = (bf16[2,12,256]{2,1,0:T(8,128)(2,1)S(1)}, bf16[2,12,256]{2,1,0:T(8,128)(2,1)S(1)}, u32[]{:S(2)}, u32[]{:S(2)}) collective-permute-start(bf16[2,12,256]{2,1,0:T(8,128)(2,1)S(1)} %get-tuple-element.299), channel_id=1, source_target_pairs={{8,0},{16,8},{24,16},{32,24},{40,32},{48,40},{56,48},{64,56},{72,6... | collective-permute-start | bytes 36872 | tf_op jit(solution)/shard_map/while/body/eval_jaxpr/ppermute | solution.py:12
  654.0 9.0 collective-permute-start
  679.0 20.6 %collective-permute-start.1 = (bf16[2,12,256]{2,1,0:T(8,128)(2,1)S(1)}, bf16[2,12,256]{2,1,0:T(8,128)(2,1)S(1)}, u32[]{:S(2)}, u32[]{:S(2)}) collective-permute-start(bf16[2,12,256]{2,1,0:T(8,128)(2,1)S(1)} %get-tuple-element.299), channel_id=1, source_target_pairs={{8,0},{16,8},{24,16},{32,24},{40,32},{48,40},{56,48},{64,56},{72,6... | collective-permute-start | bytes 36872 | tf_op jit(solution)/shard_map/while/body/eval_jaxpr/ppermute | solution.py:12
  720.2 20.6 %collective-permute-start.1 = (bf16[2,12,256]{2,1,0:T(8,128)(2,1)S(1)}, bf16[2,12,256]{2,1,0:T(8,128)(2,1)S(1)}, u32[]{:S(2)}, u32[]{:S(2)}) collective-permute-start(bf16[2,12,256]{2,1,0:T(8,128)(2,1)S(1)} %get-tuple-element.299), channel_id=1, source_target_pairs={{8,0},{16,8},{24,16},{32,24},{40,32},{48,40},{56,48},{64,56},{72,6... | collective-permute-start | bytes 36872 | tf_op jit(solution)/shard_map/while/body/eval_jaxpr/ppermute | solution.py:12
  761.4 20.6 %collective-permute-start.1 = (bf16[2,12,256]{2,1,0:T(8,128)(2,1)S(1)}, bf16[2,12,256]{2,1,0:T(8,128)(2,1)S(1)}, u32[]{:S(2)}, u32[]{:S(2)}) collective-permute-start(bf16[2,12,256]{2,1,0:T(8,128)(2,1)S(1)} %get-tuple-element.299), channel_id=1, source_target_pairs={{8,0},{16,8},{24,16},{32,24},{40,32},{48,40},{56,48},{64,56},{72,6... | collective-permute-start | bytes 36872 | tf_op jit(solution)/shard_map/while/body/eval_jaxpr/ppermute | solution.py:12
  777.6 9.0 collective-permute-start
  802.6 20.6 %collective-permute-start.1 = (bf16[2,12,256]{2,1,0:T(8,128)(2,1)S(1)}, bf16[2,12,256]{2,1,0:T(8,128)(2,1)S(1)}, u32[]{:S(2)}, u32[]{:S(2)}) collective-permute-start(bf16[2,12,256]{2,1,0:T(8,128)(2,1)S(1)} %get-tuple-element.299), channel_id=1, source_target_pairs={{8,0},{16,8},{24,16},{32,24},{40,32},{48,40},{56,48},{64,56},{72,6... | collective-permute-start | bytes 36872 | tf_op jit(solution)/shard_map/while/body/eval_jaxpr/ppermute | solution.py:12
  818.9 9.0 collective-permute-start
  843.8 20.6 %collective-permute-start.1 = (bf16[2,12,256]{2,1,0:T(8,128)(2,1)S(1)}, bf16[2,12,256]{2,1,0:T(8,128)(2,1)S(1)}, u32[]{:S(2)}, u32[]{:S(2)}) collective-permute-start(bf16[2,12,256]{2,1,0:T(8,128)(2,1)S(1)} %get-tuple-element.299), channel_id=1, source_target_pairs={{8,0},{16,8},{24,16},{32,24},{40,32},{48,40},{56,48},{64,56},{72,6... | collective-permute-start | bytes 36872 | tf_op jit(solution)/shard_map/while/body/eval_jaxpr/ppermute | solution.py:12
  885.0 20.6 %collective-permute-start.1 = (bf16[2,12,256]{2,1,0:T(8,128)(2,1)S(1)}, bf16[2,12,256]{2,1,0:T(8,128)(2,1)S(1)}, u32[]{:S(2)}, u32[]{:S(2)}) collective-permute-start(bf16[2,12,256]{2,1,0:T(8,128)(2,1)S(1)} %get-tuple-element.299), channel_id=1, source_target_pairs={{8,0},{16,8},{24,16},{32,24},{40,32},{48,40},{56,48},{64,56},{72,6... | collective-permute-start | bytes 36872 | tf_op jit(solution)/shard_map/while/body/eval_jaxpr/ppermute | solution.py:12
  926.2 20.6 %collective-permute-start.1 = (bf16[2,12,256]{2,1,0:T(8,128)(2,1)S(1)}, bf16[2,12,256]{2,1,0:T(8,128)(2,1)S(1)}, u32[]{:S(2)}, u32[]{:S(2)}) collective-permute-start(bf16[2,12,256]{2,1,0:T(8,128)(2,1)S(1)} %get-tuple-element.299), channel_id=1, source_target_pairs={{8,0},{16,8},{24,16},{32,24},{40,32},{48,40},{56,48},{64,56},{72,6... | collective-permute-start | bytes 36872 | tf_op jit(solution)/shard_map/while/body/eval_jaxpr/ppermute | solution.py:12
  967.4 20.5 %collective-permute-start.1 = (bf16[2,12,256]{2,1,0:T(8,128)(2,1)S(1)}, bf16[2,12,256]{2,1,0:T(8,128)(2,1)S(1)}, u32[]{:S(2)}, u32[]{:S(2)}) collective-permute-start(bf16[2,12,256]{2,1,0:T(8,128)(2,1)S(1)} %get-tuple-element.299), channel_id=1, source_target_pairs={{8,0},{16,8},{24,16},{32,24},{40,32},{48,40},{56,48},{64,56},{72,6... | collective-permute-start | bytes 36872 | tf_op jit(solution)/shard_map/while/body/eval_jaxpr/ppermute | solution.py:12
  1008.6 20.5 %collective-permute-start.1 = (bf16[2,12,256]{2,1,0:T(8,128)(2,1)S(1)}, bf16[2,12,256]{2,1,0:T(8,128)(2,1)S(1)}, u32[]{:S(2)}, u32[]{:S(2)}) collective-permute-start(bf16[2,12,256]{2,1,0:T(8,128)(2,1)S(1)} %get-tuple-element.299), channel_id=1, source_target_pairs={{8,0},{16,8},{24,16},{32,24},{40,32},{48,40},{56,48},{64,56},{72,6... | collective-permute-start | bytes 36872 | tf_op jit(solution)/shard_map/while/body/eval_jaxpr/ppermute | solution.py:12
  1024.8 9.0 collective-permute-start
  1049.8 20.5 %collective-permute-start.1 = (bf16[2,12,256]{2,1,0:T(8,128)(2,1)S(1)}, bf16[2,12,256]{2,1,0:T(8,128)(2,1)S(1)}, u32[]{:S(2)}, u32[]{:S(2)}) collective-permute-start(bf16[2,12,256]{2,1,0:T(8,128)(2,1)S(1)} %get-tuple-element.299), channel_id=1, source_target_pairs={{8,0},{16,8},{24,16},{32,24},{40,32},{48,40},{56,48},{64,56},{72,6... | collective-permute-start | bytes 36872 | tf_op jit(solution)/shard_map/while/body/eval_jaxpr/ppermute | solution.py:12
  1066.0 9.0 collective-permute-start
  1090.9 20.5 %collective-permute-start.1 = (bf16[2,12,256]{2,1,0:T(8,128)(2,1)S(1)}, bf16[2,12,256]{2,1,0:T(8,128)(2,1)S(1)}, u32[]{:S(2)}, u32[]{:S(2)}) collective-permute-start(bf16[2,12,256]{2,1,0:T(8,128)(2,1)S(1)} %get-tuple-element.299), channel_id=1, source_target_pairs={{8,0},{16,8},{24,16},{32,24},{40,32},{48,40},{56,48},{64,56},{72,6... | collective-permute-start | bytes 36872 | tf_op jit(solution)/shard_map/while/body/eval_jaxpr/ppermute | solution.py:12
  1132.1 20.5 %collective-permute-start.1 = (bf16[2,12,256]{2,1,0:T(8,128)(2,1)S(1)}, bf16[2,12,256]{2,1,0:T(8,128)(2,1)S(1)}, u32[]{:S(2)}, u32[]{:S(2)}) collective-permute-start(bf16[2,12,256]{2,1,0:T(8,128)(2,1)S(1)} %get-tuple-element.299), channel_id=1, source_target_pairs={{8,0},{16,8},{24,16},{32,24},{40,32},{48,40},{56,48},{64,56},{72,6... | collective-permute-start | bytes 36872 | tf_op jit(solution)/shard_map/while/body/eval_jaxpr/ppermute | solution.py:12
  1148.3 9.0 collective-permute-start
  1173.3 20.5 %collective-permute-start.1 = (bf16[2,12,256]{2,1,0:T(8,128)(2,1)S(1)}, bf16[2,12,256]{2,1,0:T(8,128)(2,1)S(1)}, u32[]{:S(2)}, u32[]{:S(2)}) collective-permute-start(bf16[2,12,256]{2,1,0:T(8,128)(2,1)S(1)} %get-tuple-element.299), channel_id=1, source_target_pairs={{8,0},{16,8},{24,16},{32,24},{40,32},{48,40},{56,48},{64,56},{72,6... | collective-permute-start | bytes 36872 | tf_op jit(solution)/shard_map/while/body/eval_jaxpr/ppermute | solution.py:12
  1189.5 9.0 collective-permute-start
  1214.5 20.5 %collective-permute-start.1 = (bf16[2,12,256]{2,1,0:T(8,128)(2,1)S(1)}, bf16[2,12,256]{2,1,0:T(8,128)(2,1)S(1)}, u32[]{:S(2)}, u32[]{:S(2)}) collective-permute-start(bf16[2,12,256]{2,1,0:T(8,128)(2,1)S(1)} %get-tuple-element.299), channel_id=1, source_target_pairs={{8,0},{16,8},{24,16},{32,24},{40,32},{48,40},{56,48},{64,56},{72,6... | collective-permute-start | bytes 36872 | tf_op jit(solution)/shard_map/while/body/eval_jaxpr/ppermute | solution.py:12
  1230.7 9.0 collective-permute-start
  1255.6 20.5 %collective-permute-start.1 = (bf16[2,12,256]{2,1,0:T(8,128)(2,1)S(1)}, bf16[2,12,256]{2,1,0:T(8,128)(2,1)S(1)}, u32[]{:S(2)}, u32[]{:S(2)}) collective-permute-start(bf16[2,12,256]{2,1,0:T(8,128)(2,1)S(1)} %get-tuple-element.299), channel_id=1, source_target_pairs={{8,0},{16,8},{24,16},{32,24},{40,32},{48,40},{56,48},{64,56},{72,6... | collective-permute-start | bytes 36872 | tf_op jit(solution)/shard_map/while/body/eval_jaxpr/ppermute | solution.py:12
  1296.8 20.5 %collective-permute-start.1 = (bf16[2,12,256]{2,1,0:T(8,128)(2,1)S(1)}, bf16[2,12,256]{2,1,0:T(8,128)(2,1)S(1)}, u32[]{:S(2)}, u32[]{:S(2)}) collective-permute-start(bf16[2,12,256]{2,1,0:T(8,128)(2,1)S(1)} %get-tuple-element.299), channel_id=1, source_target_pairs={{8,0},{16,8},{24,16},{32,24},{40,32},{48,40},{56,48},{64,56},{72,6... | collective-permute-start | bytes 36872 | tf_op jit(solution)/shard_map/while/body/eval_jaxpr/ppermute | solution.py:12
  1338.0 20.5 %collective-permute-start.1 = (bf16[2,12,256]{2,1,0:T(8,128)(2,1)S(1)}, bf16[2,12,256]{2,1,0:T(8,128)(2,1)S(1)}, u32[]{:S(2)}, u32[]{:S(2)}) collective-permute-start(bf16[2,12,256]{2,1,0:T(8,128)(2,1)S(1)} %get-tuple-element.299), channel_id=1, source_target_pairs={{8,0},{16,8},{24,16},{32,24},{40,32},{48,40},{56,48},{64,56},{72,6... | collective-permute-start | bytes 36872 | tf_op jit(solution)/shard_map/while/body/eval_jaxpr/ppermute | solution.py:12
  1354.2 9.0 collective-permute-start
  1379.2 20.5 %collective-permute-start.1 = (bf16[2,12,256]{2,1,0:T(8,128)(2,1)S(1)}, bf16[2,12,256]{2,1,0:T(8,128)(2,1)S(1)}, u32[]{:S(2)}, u32[]{:S(2)}) collective-permute-start(bf16[2,12,256]{2,1,0:T(8,128)(2,1)S(1)} %get-tuple-element.299), channel_id=1, source_target_pairs={{8,0},{16,8},{24,16},{32,24},{40,32},{48,40},{56,48},{64,56},{72,6... | collective-permute-start | bytes 36872 | tf_op jit(solution)/shard_map/while/body/eval_jaxpr/ppermute | solution.py:12
  1420.3 20.5 %collective-permute-start.1 = (bf16[2,12,256]{2,1,0:T(8,128)(2,1)S(1)}, bf16[2,12,256]{2,1,0:T(8,128)(2,1)S(1)}, u32[]{:S(2)}, u32[]{:S(2)}) collective-permute-start(bf16[2,12,256]{2,1,0:T(8,128)(2,1)S(1)} %get-tuple-element.299), channel_id=1, source_target_pairs={{8,0},{16,8},{24,16},{32,24},{40,32},{48,40},{56,48},{64,56},{72,6... | collective-permute-start | bytes 36872 | tf_op jit(solution)/shard_map/while/body/eval_jaxpr/ppermute | solution.py:12
  1461.5 20.5 %collective-permute-start.1 = (bf16[2,12,256]{2,1,0:T(8,128)(2,1)S(1)}, bf16[2,12,256]{2,1,0:T(8,128)(2,1)S(1)}, u32[]{:S(2)}, u32[]{:S(2)}) collective-permute-start(bf16[2,12,256]{2,1,0:T(8,128)(2,1)S(1)} %get-tuple-element.299), channel_id=1, source_target_pairs={{8,0},{16,8},{24,16},{32,24},{40,32},{48,40},{56,48},{64,56},{72,6... | collective-permute-start | bytes 36872 | tf_op jit(solution)/shard_map/while/body/eval_jaxpr/ppermute | solution.py:12
  1477.7 9.0 collective-permute-start
  1502.7 20.5 %collective-permute-start.1 = (bf16[2,12,256]{2,1,0:T(8,128)(2,1)S(1)}, bf16[2,12,256]{2,1,0:T(8,128)(2,1)S(1)}, u32[]{:S(2)}, u32[]{:S(2)}) collective-permute-start(bf16[2,12,256]{2,1,0:T(8,128)(2,1)S(1)} %get-tuple-element.299), channel_id=1, source_target_pairs={{8,0},{16,8},{24,16},{32,24},{40,32},{48,40},{56,48},{64,56},{72,6... | collective-permute-start | bytes 36872 | tf_op jit(solution)/shard_map/while/body/eval_jaxpr/ppermute | solution.py:12
  1518.9 9.0 collective-permute-start
  1543.9 20.5 %collective-permute-start.1 = (bf16[2,12,256]{2,1,0:T(8,128)(2,1)S(1)}, bf16[2,12,256]{2,1,0:T(8,128)(2,1)S(1)}, u32[]{:S(2)}, u32[]{:S(2)}) collective-permute-start(bf16[2,12,256]{2,1,0:T(8,128)(2,1)S(1)} %get-tuple-element.299), channel_id=1, source_target_pairs={{8,0},{16,8},{24,16},{32,24},{40,32},{48,40},{56,48},{64,56},{72,6... | collective-permute-start | bytes 36872 | tf_op jit(solution)/shard_map/while/body/eval_jaxpr/ppermute | solution.py:12
  1560.1 9.0 collective-permute-start
  1585.0 20.5 %collective-permute-start.1 = (bf16[2,12,256]{2,1,0:T(8,128)(2,1)S(1)}, bf16[2,12,256]{2,1,0:T(8,128)(2,1)S(1)}, u32[]{:S(2)}, u32[]{:S(2)}) collective-permute-start(bf16[2,12,256]{2,1,0:T(8,128)(2,1)S(1)} %get-tuple-element.299), channel_id=1, source_target_pairs={{8,0},{16,8},{24,16},{32,24},{40,32},{48,40},{56,48},{64,56},{72,6... | collective-permute-start | bytes 36872 | tf_op jit(solution)/shard_map/while/body/eval_jaxpr/ppermute | solution.py:12
  (55 other events, 1327.6 us)
where the time goes:
time: 1620 us; the launch traced here: 1610 us
  blocking collectives  1000 us (62%)
  starting transfers between devices  228 us (14%)
  waiting for transfers between devices  183 us (11%)
  matrix products  118 us (7%)
  other arithmetic  60.6 us (4%)
    all_gather x39, blocking collectives, loop_body(): lax.all_gather(piece_up, 'iface', axis=2, tiled=True)  503 us
    all_gather x39, blocking collectives, loop_body(): lax.all_gather(piece_down, 'iface', axis=2, tiled=True)  498 us
    ppermute x78, starting transfers between devices, shifted(): return lax.ppermute(block, axis, route)  228 us
    ppermute x78, waiting for transfers between devices, shifted(): return lax.ppermute(block, axis, route)  183 us
    dot_general x78, matrix products, complex_apply(): lax.dot_general(traces, matrix, (((2,), (2,)), ((), ())), preferred_eleme...  118 us
    select_n x78, other arithmetic, advance(): jnp.where(is_valid, fresh, previous)  59.2 us
  transfers between devices with their start and end apart: 78, of which 39 were waited for; matrix products, arithmetic and copies ran while one was open for 5% of the time, Pallas kernels for 0%

commit v1 on v0

v1 whole, which is shorter than its diff:
```python
import functools

import jax
import jax.numpy as jnp
from jax import lax
from jax.experimental import pallas as pl
from jax.experimental.pallas import tpu as pltpu
from jax.sharding import PartitionSpec as P

MESH = pl.DeviceIdType.MESH
LAYERS = 32
Y = 4
ROWS = 256
PIECE = 2 * ROWS
BATCHES = 12
LAG = 5


def kernel(
    batches, gd_ref, gu_ref, sd_ref, su_ref, o_ref,
    graw, gt, src, ins, outs,
    g_sem, gt_send, gt_recv, src_send, src_recv, send_sem, recv_sem, half_send, half_recv, o_sem,
):
    shots = sd_ref.shape[2]
    width = shots // batches
    layer = lax.axis_index("layer")
    iface = lax.axis_index("iface")
    y, core = iface // 2, lax.rem(iface, 2)
    sibling = (layer, 2 * y + 1 - core)
    first = jnp.where(layer < LAYERS // 2, 0, 1)
    second = 1 - first

    def load(d):
        def start(ref, at):
            pltpu.make_async_copy(ref.at[0], graw.at[at], g_sem.at[at]).start()

        @pl.when(d == 0)
        def _():
            start(gd_ref, 0)

        @pl.when(d == 1)
        def _():
            start(gu_ref, 1)

    def load_wait(d):
        pltpu.make_async_copy(gd_ref.at[0], graw.at[d], g_sem.at[d]).wait()

    def place_source(c):
        for d, ref in ((0, sd_ref), (1, su_ref)):
            for b in range(batches):
                rows = [ref[0, p, b * width : (b + 1) * width, :].astype(jnp.float32) for p in range(2)]
                src[d, b, :, c * ROWS : (c + 1) * ROWS] = jnp.concatenate(rows, 0).astype(jnp.bfloat16)

    def transpose(d, p, q, c):
        block = graw[d, p, :, pl.ds(pl.multiple_of(q * PIECE, PIECE), PIECE)]
        gt[d, q, :, p * PIECE + c * ROWS : p * PIECE + (c + 1) * ROWS] = block.T

    def gt_copy(d, p, q):
        cols = pl.ds(p * PIECE, ROWS)
        return pltpu.make_async_remote_copy(
            gt.at[d, q, :, cols], gt.at[d, q, :, cols], gt_send.at[d, p, q], gt_recv.at[d, p, q],
            device_id=sibling, device_id_type=MESH,
        )

    def src_copy(d):
        half = src.at[d, :, :, pl.ds(0, ROWS)]
        return pltpu.make_async_remote_copy(
            half, half, src_send.at[d], src_recv.at[d], device_id=sibling, device_id_type=MESH
        )

    def half_copy(d, b):
        half = outs.at[d, b, :, pl.ds(0, ROWS)]
        return pltpu.make_async_remote_copy(
            half, half, half_send.at[d, b], half_recv.at[d, b], device_id=sibling, device_id_type=MESH
        )

    def out_copy(d, b, c):
        return pltpu.make_async_copy(outs.at[d, b, :, pl.ds(c * ROWS, ROWS)], o_ref.at[d, b], o_sem.at[d, b])

    middle = (layer == LAYERS // 2 - 1) | (layer == LAYERS // 2)
    lead = jnp.where(middle, LAG, batches)

    def item(k):
        j = k - lead
        mixed = 2 * (batches - lead)
        in_lead, in_mixed = k < lead, j < mixed
        odd = lax.rem(jnp.maximum(j, 0), 2)
        half = jnp.maximum(j, 0) // 2
        d = jnp.where(in_lead, first, jnp.where(in_mixed, jnp.where(odd == 1, first, second), second))
        b = jnp.where(in_lead, k, jnp.where(in_mixed, jnp.where(odd == 1, lead + half, half), k - batches))
        return d, b

    load(first)
    load(second)
    barrier = pltpu.get_barrier_semaphore()
    pl.semaphore_signal(barrier, 1, device_id=sibling, device_id_type=MESH)

    @pl.when(core == 0)
    def _():
        place_source(0)
        pl.semaphore_wait(barrier, 1)
        src_copy(0).start()
        src_copy(1).start()
        for d in (first, second):
            load_wait(d)
            for p in range(2):

                def step(q, carry):
                    transpose(d, p, q, 0)
                    gt_copy(d, p, q).start()
                    return carry

                lax.fori_loop(0, Y, step, 0)

        def sent(k, carry):
            d, b = item(k)
            half_copy(d, b).wait_recv()
            out_copy(d, b, 0).start()
            return carry

        lax.fori_loop(0, 2 * batches, sent, 0)
        for d in range(2):
            src_copy(d).wait_send()
            for p in range(2):
                for q in range(Y):
                    gt_copy(d, p, q).wait_send()

        def written(k, carry):
            d, b = item(k)
            out_copy(d, b, 0).wait()
            return carry

        lax.fori_loop(0, 2 * batches, written, 0)

    @pl.when(core == 1)
    def _():
        above, below = lax.rem(layer + LAYERS - 1, LAYERS), lax.rem(layer + 1, LAYERS)
        for other in (above, below):
            for q in range(Y):
                pl.semaphore_signal(barrier, 1, device_id=(other, 2 * q + 1), device_id_type=MESH)
        place_source(1)
        pl.semaphore_wait(barrier, 1 + 2 * Y)
        src_copy(0).wait_recv()
        src_copy(1).wait_recv()

        def position(d):
            return jnp.where(d == 0, layer, LAYERS - 1 - layer)

        def prepare(d):
            load_wait(d)
            for p in range(2):

                def step(q, carry):
                    transpose(d, p, q, 1)
                    return carry

                lax.fori_loop(0, Y, step, 0)
            for p in range(2):
                for q in range(Y):
                    gt_copy(d, p, q).wait_recv()

        def send(d, b, off):
            to = (jnp.where(d == 0, below, above), 2 * lax.rem(y + off, Y) + 1)
            return pltpu.make_async_remote_copy(
                outs.at[d, b], ins.at[d, b, y], send_sem.at[d, b, off], recv_sem.at[d, b, y],
                device_id=to, device_id_type=MESH,
            )

        def arrival(d, b, q):
            return pltpu.make_async_remote_copy(
                outs.at[d, b], ins.at[d, b, q], send_sem.at[d, b, 0], recv_sem.at[d, b, q],
                device_id=sibling, device_id_type=MESH,
            )

        edge = (layer == 0) | (layer == LAYERS - 1)
        late = jnp.where((layer < LAYERS // 4) | (layer >= LAYERS - LAYERS // 4), batches, 0)

        @pl.when(jnp.logical_not(edge))
        def _():
            prepare(first)

        def step(k, carry):
            d, b = item(k)
            pos = position(d)

            @pl.when(k == late)
            def _():
                prepare(second)

            @pl.when(pos == 0)
            def _():
                outs[d, b] = src[d, b]

            @pl.when(pos > 0)
            def _():
                total = None
                for off in (0, 1, 3, 2):
                    q = lax.rem(y + off, Y)
                    arrival(d, b, q).wait_recv()
                    part = jnp.dot(ins[d, b, q], gt[d, q], preferred_element_type=jnp.float32)
                    total = part if total is None else total + part
                real = total[:width, :PIECE] - total[width:, PIECE:]
                imag = total[:width, PIECE:] + total[width:, :PIECE]
                fresh = jnp.concatenate([real, imag], 0) + src[d, b].astype(jnp.float32)
                outs[d, b] = fresh.astype(jnp.bfloat16)

            @pl.when(pos < LAYERS - 1)
            def _():
                for off in (2, 1, 3, 0):
                    send(d, b, off).start()

            half_copy(d, b).start()
            out_copy(d, b, 1).start()
            return carry

        lax.fori_loop(0, 2 * batches, step, 0)

        @pl.when(edge)
        def _():
            prepare(first)

        def finish(k, carry):
            d, b = item(k)

            @pl.when(position(d) < LAYERS - 1)
            def _():
                for off in range(Y):
                    send(d, b, off).wait_send()

            half_copy(d, b).wait_send()
            out_copy(d, b, 1).wait()
            return carry

        lax.fori_loop(0, 2 * batches, finish, 0)


def on_device(green_down, green_up, source_down, source_up):
    shots = source_down.shape[2]
    width = shots // BATCHES
    points = green_down.shape[3]
    any_space = pl.BlockSpec(memory_space=pl.ANY)
    vmem = pl.BlockSpec(memory_space=pltpu.VMEM)
    dma = pltpu.SemaphoreType.DMA
    out = pl.pallas_call(
        functools.partial(kernel, BATCHES),
        out_shape=jax.ShapeDtypeStruct((2, BATCHES, 2 * width, ROWS), jnp.bfloat16),
        in_specs=[any_space, any_space, vmem, vmem],
        out_specs=any_space,
        scratch_shapes=[
            pltpu.VMEM((2, 2, ROWS, points), jnp.bfloat16),
            pltpu.VMEM((2, Y, PIECE, 2 * PIECE), jnp.bfloat16),
            pltpu.VMEM((2, BATCHES, 2 * width, PIECE), jnp.bfloat16),
            pltpu.VMEM((2, BATCHES, Y, 2 * width, PIECE), jnp.bfloat16),
            pltpu.VMEM((2, BATCHES, 2 * width, PIECE), jnp.bfloat16),
            dma((2,)),
            dma((2, 2, Y)),
            dma((2, 2, Y)),
            dma((2,)),
            dma((2,)),
            dma((2, BATCHES, Y)),
            dma((2, BATCHES, Y)),
            dma((2, BATCHES)),
            dma((2, BATCHES)),
            dma((2, BATCHES)),
        ],
        compiler_params=pltpu.CompilerParams(
            collective_id=0, has_side_effects=True, vmem_limit_bytes=40 << 20
        ),
    )(green_down, green_up, source_down, source_up)
    out = out.reshape(2, BATCHES, 2, width, ROWS).transpose(0, 2, 1, 3, 4).reshape(2, 2, shots, ROWS)
    return out[0][None], out[1][None]


def solution(mesh):
    in_specs = (
        P("layer", None, "iface", None),
        P("layer", None, "iface", None),
        P("layer", None, None, "iface"),
        P("layer", None, None, "iface"),
    )
    out_specs = (P("layer", None, None, "iface"), P("layer", None, None, "iface"))
    return jax.shard_map(
        on_device, mesh=mesh, in_specs=in_specs, out_specs=out_specs, check_vma=False
    )
```

time: 1620 us -> 161 us (0.10)
  the two profiles are of different devices: /device:TPU:128 before, /device:TPU:1 now
where the time goes in v1:
time: 161 us
  Pallas kernels  154 us (96%)
  local copies, waits for them, and re-layouts  5.66 us (4%)
    pallas_call x1, Pallas kernels, on_device(): pl.pallas_call(functools.partial(kernel, BATCHES), out_shape=jax.ShapeDty...  154 us
    unnamed x8, local copies, waits for them, and re-layouts  4.96 us

profile of v1, /device:TPU:1, one launch (start us, length us, event | category | flops | bytes accessed | tf_op | source)
XLA Modules:
  0.0 160.8 jit_solution(13565805896264517232)
XLA Ops:
  0.6 0.0 copy-start
  0.6 1.6 copy-done
  2.2 0.0 copy-start.1
  2.2 1.6 copy-done.1
  3.8 0.0 copy-start.2
  3.8 0.9 copy-done.2
  4.7 0.0 copy-start.3
  4.7 0.9 copy-done.3
  5.6 154.4 %shard_map.59 = bf16[2,12,16,256]{3,2,1,0:T(8,128)(2,1)S(1)} custom-call(bf16[1,2,256,2048]{3,2,1,0:T(8,128)(2,1)S(1)} %copy-done, bf16[1,2,256,2048]{3,2,1,0:T(8,128)(2,1)S(1)} %copy-done.1, bf16[1,2,96,256]{3,2,1,0:T(8,128)(2,1)S(1)} %copy-done.2, bf16[1,2,96,256]{3,2,1,0:T(8,128)(2,1)S(1)} %copy-done.3), custom_call_target="tpu_custom_call" | custom-call | tf_op jit(solution)/shard_map/pallas_call | solution.py:244
  160.1 0.7 copy_bitcast_fusion
  (1 shorter events, 0.0 us)
Async XLA Ops:
  0.6 1.6 copy-start
  2.2 1.6 copy-start.1
  3.8 0.9 copy-start.2
  4.7 0.9 copy-start.3

commit v2 on v1

--- a/solution.py
+++ b/solution.py
@@ -12,8 +12,9 @@
 Y = 4
 ROWS = 256
 PIECE = 2 * ROWS
+SIDE = 256
 BATCHES = 12
-LAG = 5
+LAG = 8
 
 
 def kernel(
@@ -187,22 +188,54 @@
             def _():
                 prepare(second)
 
+            @pl.when(edge & (k == late))
+            def _():
+                load_wait(first)
+                for p in range(2):
+                    for q in range(Y):
+                        gt_copy(first, p, q).wait_recv()
+
             @pl.when(pos == 0)
             def _():
                 outs[d, b] = src[d, b]
 
             @pl.when(pos > 0)
             def _():
-                total = None
-                for off in (0, 1, 3, 2):
-                    q = lax.rem(y + off, Y)
-                    arrival(d, b, q).wait_recv()
-                    part = jnp.dot(ins[d, b, q], gt[d, q], preferred_element_type=jnp.float32)
-                    total = part if total is None else total + part
-                real = total[:width, :PIECE] - total[width:, PIECE:]
-                imag = total[:width, PIECE:] + total[width:, :PIECE]
-                fresh = jnp.concatenate([real, imag], 0) + src[d, b].astype(jnp.float32)
-                outs[d, b] = fresh.astype(jnp.bfloat16)
+                def run(*sums):
+                    order = [lax.rem(y + off, Y) for off in (0, 1, 3, 2)]
+
+                    def push(q, t):
+                        rows = slice(t // 2 * SIDE, (t // 2 + 1) * SIDE)
+                        for m in range(2):
+                            at = (2 * m + t % 2) * SIDE
+                            pltpu.matmul_push_rhs(gt[d, q, rows, at : at + SIDE], t % 2, m)
+
+                    def multiply(block, t):
+                        cols = slice(t // 2 * SIDE, (t // 2 + 1) * SIDE)
+                        for m in range(2):
+                            pltpu.matmul_acc_lhs(sums[2 * m + t % 2], block[:, cols], t % 2)
+
+                    push(order[0], 0)
+                    push(order[0], 1)
+                    for n, q in enumerate(order):
+                        arrival(d, b, q).wait_recv()
+                        block = ins[d, b, q]
+                        for t in range(4):
+                            multiply(block, t)
+                            if t < 2:
+                                push(q, t + 2)
+                            elif n + 1 < Y:
+                                push(order[n + 1], t - 2)
+                    for h in range(2):
+                        by_real, by_imag = pltpu.matmul_pop(sums[h]), pltpu.matmul_pop(sums[2 + h])
+                        real = by_real[:width] - by_imag[width:]
+                        imag = by_imag[:width] + by_real[width:]
+                        cols = slice(h * SIDE, (h + 1) * SIDE)
+                        fresh = jnp.concatenate([real, imag], 0) + src[d, b, :, cols].astype(jnp.float32)
+                        outs[d, b, :, cols] = fresh.astype(jnp.bfloat16)
+
+                scratch = [pltpu.ACC(mxu_id=n // 2)((2 * width, SIDE), jnp.float32) for n in range(4)]
+                pl.run_scoped(run, *scratch)
 
             @pl.when(pos < LAYERS - 1)
             def _():
@@ -214,10 +247,6 @@
             return carry
 
         lax.fori_loop(0, 2 * batches, step, 0)
-
-        @pl.when(edge)
-        def _():
-            prepare(first)
 
         def finish(k, carry):
             d, b = item(k)
@@ -264,7 +293,7 @@
             dma((2, BATCHES)),
         ],
         compiler_params=pltpu.CompilerParams(
-            collective_id=0, has_side_effects=True, vmem_limit_bytes=40 << 20
+            collective_id=0, has_side_effects=True, vmem_limit_bytes=60 << 20
         ),
     )(green_down, green_up, source_down, source_up)
     out = out.reshape(2, BATCHES, 2, width, ROWS).transpose(0, 2, 1, 3, 4).reshape(2, 2, shots, ROWS)

time: 161 us -> 150 us (0.932)
  Pallas kernels: 154 us -> 147 us
  local copies, waits for them, and re-layouts: 5.66 us -> 1.64 us
    pallas_call x1, Pallas kernels: 154 us -> 147 us  [on_device(): pl.pallas_call(functools.partial(kernel, BATCHES), out_shape=jax.ShapeDty...]
    unnamed x8 -> x0, local copies, waits for them, and re-layouts: 4.96 us -> none
where the time goes in v2:
time: 150 us; the launch traced here: 149 us
  Pallas kernels  147 us (98%)
  local copies, waits for them, and re-layouts  1.64 us (1%)
    pallas_call x1, Pallas kernels, on_device(): pl.pallas_call(functools.partial(kernel, BATCHES), out_shape=jax.ShapeDty...  147 us

profile of v2, /device:TPU:1, one launch (start us, length us, event | category | flops | bytes accessed | tf_op | source)
XLA Modules:
  0.0 149.5 jit_solution(12196370928067624476)
XLA Ops:
  0.6 147.2 %shard_map.59 = bf16[2,12,16,256]{3,2,1,0:T(8,128)(2,1)} custom-call(bf16[1,2,256,2048]{3,2,1,0:T(8,128)(2,1)} %gd_ref.1, bf16[1,2,256,2048]{3,2,1,0:T(8,128)(2,1)} %gu_ref.1, bf16[1,2,96,256]{3,2,1,0:T(8,128)(2,1)} %sd_ref.1, bf16[1,2,96,256]{3,2,1,0:T(8,128)(2,1)} %su_ref.1), custom_call_target="tpu_custom_call" | custom-call | tf_op jit(solution)/shard_map/pallas_call | solution.py:273
  147.8 1.0 fusion
  148.8 0.7 copy_bitcast_fusion

commit v3 on v0

v3 whole, which is shorter than its diff:
```python
import functools

import jax
import jax.numpy as jnp
from jax import lax
from jax.experimental import pallas as pl
from jax.experimental.pallas import tpu as pltpu
from jax.sharding import PartitionSpec as P

MESH = pl.DeviceIdType.MESH
LAYERS = 32
LAST = LAYERS - 1
MID = LAYERS // 2
Y = 4
ROWS = 256
PIECE = 2 * ROWS
SIDE = 256
BATCHES = 12
SENDS = Y + 1


def kernel(
    batches, gd_ref, gu_ref, sd_ref, su_ref, o_ref,
    graw, sraw, gt, src, ins, outs,
    g_sem, s_sem, gt_send, gt_recv, src_send, src_recv, send_sem, recv_sem, half_send, half_recv, o_sem,
):
    shots = sd_ref.shape[2]
    width = shots // batches
    layer = lax.axis_index("layer")
    iface = lax.axis_index("iface")
    y, core = iface // 2, lax.rem(iface, 2)
    sibling = (layer, 2 * y + 1 - core)
    first = jnp.where(layer < MID, 0, 1)
    second = 1 - first
    middle = (layer == MID - 1) | (layer == MID)
    central = (layer >= MID // 2) & (layer < LAYERS - MID // 2)

    def worker_of(at, d):
        return jnp.where(((at == MID - 1) | (at == MID)) & (d == 0), 0, 1)

    def position(d):
        return jnp.where(d == 0, layer, LAST - layer)

    def load(d):
        def start(ref, at):
            for p in range(2):
                pltpu.make_async_copy(ref.at[0, p], graw.at[at, p], g_sem.at[at, p]).start()

        @pl.when(d == 0)
        def _():
            start(gd_ref, 0)

        @pl.when(d == 1)
        def _():
            start(gu_ref, 1)

    def load_wait(d, p):
        pltpu.make_async_copy(gd_ref.at[0, p], graw.at[d, p], g_sem.at[d, p]).wait()

    def source_load(d):
        ref = (sd_ref, su_ref)[d]
        return pltpu.make_async_copy(ref.at[0], sraw.at[d], s_sem.at[d])

    def place_source(c):
        for d in range(2):
            source_load(d).wait()
            for b in range(batches):
                rows = [sraw[d, p, b * width : (b + 1) * width, :].astype(jnp.float32) for p in range(2)]
                src[d, b, :, c * ROWS : (c + 1) * ROWS] = jnp.concatenate(rows, 0).astype(jnp.bfloat16)

    def transpose(d, c, then=None):
        for p in range(2):
            load_wait(d, p)

            def step(q, carry):
                block = graw[d, p, :, pl.ds(pl.multiple_of(q * PIECE, PIECE), PIECE)]
                gt[d, q, :, p * PIECE + c * ROWS : p * PIECE + (c + 1) * ROWS] = block.T
                if then is not None:
                    then(p, q)
                return carry

            lax.fori_loop(0, Y, step, 0)

    def remote(a, b, send, recv, to):
        return pltpu.make_async_remote_copy(a, b, send, recv, device_id=to, device_id_type=MESH)

    def gt_copy(d, c, p, q):
        half = gt.at[d, q, :, pl.ds(p * PIECE + c * ROWS, ROWS)]
        return remote(half, half, gt_send.at[d, p, q], gt_recv.at[d, p, q], sibling)

    def for_gt(act, d, c):
        for p in range(2):
            for q in range(Y):
                act(gt_copy(d, c, p, q))

    def src_copy(d, c):
        half = src.at[d, :, :, pl.ds(c * ROWS, ROWS)]
        return remote(half, half, src_send.at[d], src_recv.at[d], sibling)

    def half_copy(d, b, c):
        half = outs.at[d, b, :, pl.ds((1 - c) * ROWS, ROWS)]
        return remote(half, o_ref.at[d, b], half_send.at[d, b], half_recv.at[d, b], sibling)

    def out_copy(d, b, c):
        return pltpu.make_async_copy(outs.at[d, b, :, pl.ds(c * ROWS, ROWS)], o_ref.at[d, b], o_sem.at[d, b])

    barrier = pltpu.get_barrier_semaphore()

    def greet(at, c):
        for q in range(Y):
            pl.semaphore_signal(barrier, 1, device_id=(at, 2 * q + c), device_id_type=MESH)

    def targets(d):
        at = jnp.where(d == 0, layer + 1, layer - 1)
        worker = worker_of(at, d)
        return [(at, 2 * lax.rem(y + off, Y) + worker) for off in range(Y)]

    def send(d, b, kind, to):
        off = 2 if kind == Y else kind
        a, z = outs.at[d, b], ins.at[d, b, y]
        if off == 2:
            cols = pl.ds(SIDE if kind == Y else 0, SIDE)
            a, z = outs.at[d, b, :, cols], ins.at[d, b, y, :, cols]
        return remote(a, z, send_sem.at[d, b, kind], recv_sem.at[d, b, kind], to[off])

    def work(c, begin, end):
        def mine(d):
            return worker_of(layer, d) == c

        for d in (first, second):

            @pl.when(mine(d))
            def _():
                src_copy(d, 1 - c).wait_recv()

        @pl.when(mine(first) & (position(first) > 0))
        def _():
            for_gt(lambda copy: copy.wait_recv(), first, 1 - c)

        def drain(d):
            def step(b, carry):
                @pl.when(position(d) < LAST)
                def _():
                    for kind in range(SENDS):
                        send(d, b, kind, targets(d)).wait_send()

                half_copy(d, b, c).wait_send()
                out_copy(d, b, c).wait()
                return carry

            lax.fori_loop(0, batches, step, 0)

        def step(k, carry):
            d = jnp.where(k < batches, first, second)
            b = lax.rem(k, batches)
            pos = position(d)
            to = targets(d)

            def send_all():
                for kind in (2, Y, 1, 3, 0):
                    send(d, b, kind, to).start()

            @pl.when(k == batches)
            def _():
                if c == 1:

                    @pl.when(jnp.logical_not(central))
                    def _():
                        transpose(second, c)

                    @pl.when(begin == 0)
                    def _():
                        drain(first)

                for_gt(lambda copy: copy.wait_recv(), second, 1 - c)

            @pl.when(pos == 0)
            def _():
                outs[d, b] = src[d, b]
                send_all()

            def run(*sums):
                order = [lax.rem(y + off, Y) for off in (0, 1, 3, 2)]
                kinds = (0, 3, 1, 2)

                def push(q, t):
                    rows = slice(t // 2 * SIDE, (t // 2 + 1) * SIDE)
                    for m in range(2):
                        at = (2 * m + t % 2) * SIDE
                        pltpu.matmul_push_rhs(gt[d, q, rows, at : at + SIDE], t % 2, m)

                def arrive(n, kind):
                    part = (d, b, order[n])
                    ref = ins.at[part]
                    if kind in (2, Y):
                        ref = ins.at[(*part, slice(None), pl.ds(SIDE if kind == Y else 0, SIDE))]
                    remote(ref, ref, send_sem.at[d, b, kind], recv_sem.at[d, b, kind], sibling).wait_recv()

                push(order[0], 0)
                push(order[0], 1)
                for n, q in enumerate(order):
                    arrive(n, kinds[n])
                    for t in range(4):
                        if t == 2 and kinds[n] == 2:
                            arrive(n, Y)
                        if t % 2 == 0:
                            block = ins[d, b, q, :, t // 2 * SIDE : (t // 2 + 1) * SIDE]
                        for m in range(2):
                            pltpu.matmul_acc_lhs(sums[2 * m + t % 2], block, t % 2)
                        if t < 2:
                            push(q, t + 2)
                        elif n + 1 < Y:
                            push(order[n + 1], t - 2)
                for h in range(2):
                    by_real, by_imag = pltpu.matmul_pop(sums[h]), pltpu.matmul_pop(sums[2 + h])
                    real = by_real[:width] - by_imag[width:]
                    imag = by_imag[:width] + by_real[width:]
                    cols = slice(h * SIDE, (h + 1) * SIDE)
                    fresh = jnp.concatenate([real, imag], 0) + src[d, b, :, cols].astype(jnp.float32)
                    outs[d, b, :, cols] = fresh.astype(jnp.bfloat16)

            def compute():
                sums = [pltpu.ACC(mxu_id=n // 2)((2 * width, SIDE), jnp.float32) for n in range(4)]
                pl.run_scoped(run, *sums)

            @pl.when((pos > 0) & (pos < LAST))
            def _():
                compute()
                send_all()

            @pl.when(pos == LAST)
            def _():
                compute()

            half_copy(d, b, c).start()
            out_copy(d, b, c).start()
            return carry

        lax.fori_loop(begin, end, step, 0)
        drain(jnp.where(end == batches, first, second))

    def serve(c):
        def helps(d):
            return worker_of(layer, d) != c

        def before():
            for d in (first, second):

                @pl.when(helps(d))
                def _():
                    src_copy(d, c).start()

        def offer(d):
            def then(p, q):
                @pl.when(helps(d))
                def _():
                    gt_copy(d, c, p, q).start()

            transpose(d, c, then)

        def after():
            for d in (first, second):

                @pl.when(helps(d))
                def _():
                    def step(b, carry):
                        half_copy(d, b, 1 - c).wait_recv()
                        return carry

                    src_copy(d, c).wait_send()

                    @pl.when(position(d) > 0)
                    def _():
                        for_gt(lambda copy: copy.wait_send(), d, c)

                    lax.fori_loop(0, batches, step, 0)

        return before, offer, after

    for d in range(2):
        source_load(d).start()
    load(first)
    pl.semaphore_signal(barrier, 1, device_id=sibling, device_id_type=MESH)

    def skip(d):
        for p in range(2):
            load_wait(d, p)

    @pl.when(core == 0)
    def _():
        before, offer, after = serve(0)

        @pl.when(middle)
        def _():
            for hop in (-1, 1):
                greet(layer + hop, worker_of(layer + hop, 0))

        load(second)
        place_source(0)
        pl.semaphore_wait(barrier, 1 + jnp.where(middle, 2 * Y, 0))
        before()

        @pl.when(position(first) > 0)
        def _():
            offer(first)

        @pl.when(position(first) == 0)
        def _():
            skip(first)

        offer(second)

        @pl.when(middle)
        def _():
            begin = jnp.where(first == 0, 0, batches)
            work(0, begin, begin + batches)

        after()

    @pl.when(core == 1)
    def _():
        before, offer, after = serve(1)
        guests = 0
        for hop in (-1, 1):
            inside = (layer + hop >= 0) & (layer + hop <= LAST)
            guests = guests + jnp.where(inside, Y, 0)

            @pl.when(inside)
            def _():
                greet(layer + hop, 1)

        near = (layer == MID - 2) | (layer == MID + 1)
        guests = guests + jnp.where(near, Y, 0)

        @pl.when(near)
        def _():
            greet(jnp.where(layer < MID, MID - 1, MID), 0)

        load(second)
        place_source(1)

        @pl.when((position(first) > 0) & jnp.logical_not(middle))
        def _():
            transpose(first, 1)

        @pl.when(position(first) == 0)
        def _():
            skip(first)

        pl.semaphore_wait(barrier, 1 + guests)
        before()

        @pl.when(middle)
        def _():
            offer(first)

        @pl.when(central)
        def _():
            offer(second)

        begin = jnp.where(middle & (first == 0), batches, 0)
        work(1, begin, jnp.where(middle & (first == 1), batches, 2 * batches))
        after()


def on_device(green_down, green_up, source_down, source_up):
    shots = source_down.shape[2]
    width = shots // BATCHES
    points = green_down.shape[3]
    any_space = pl.BlockSpec(memory_space=pl.ANY)
    dma = pltpu.SemaphoreType.DMA
    trace = (BATCHES, 2 * width, PIECE)
    out = pl.pallas_call(
        functools.partial(kernel, BATCHES),
        out_shape=jax.ShapeDtypeStruct((2, BATCHES, 2 * width, ROWS), jnp.bfloat16),
        in_specs=[any_space] * 4,
        out_specs=any_space,
        scratch_shapes=[
            pltpu.VMEM((2, 2, ROWS, points), jnp.bfloat16),
            pltpu.VMEM((2, 2, shots, ROWS), jnp.bfloat16),
            pltpu.VMEM((2, Y, PIECE, 2 * PIECE), jnp.bfloat16),
            pltpu.VMEM((2, *trace), jnp.bfloat16),
            pltpu.VMEM((2, BATCHES, Y, 2 * width, PIECE), jnp.bfloat16),
            pltpu.VMEM((2, *trace), jnp.bfloat16),
            dma((2, 2)),
            dma((2,)),
            dma((2, 2, Y)),
            dma((2, 2, Y)),
            dma((2,)),
            dma((2,)),
            dma((2, BATCHES, SENDS)),
            dma((2, BATCHES, SENDS)),
            dma((2, BATCHES)),
            dma((2, BATCHES)),
            dma((2, BATCHES)),
        ],
        compiler_params=pltpu.CompilerParams(
            collective_id=0, has_side_effects=True, vmem_limit_bytes=60 << 20
        ),
    )(green_down, green_up, source_down, source_up)
    out = out.reshape(2, BATCHES, 2, width, ROWS).transpose(0, 2, 1, 3, 4).reshape(2, 2, shots, ROWS)
    return out[0][None], out[1][None]


def solution(mesh):
    in_specs = (
        P("layer", None, "iface", None),
        P("layer", None, "iface", None),
        P("layer", None, None, "iface"),
        P("layer", None, None, "iface"),
    )
    out_specs = (P("layer", None, None, "iface"), P("layer", None, None, "iface"))
    return jax.shard_map(
        on_device, mesh=mesh, in_specs=in_specs, out_specs=out_specs, check_vma=False
    )
```

time: 1620 us -> 146 us (0.09)
  the two profiles are of different devices: /device:TPU:128 before, /device:TPU:1 now
where the time goes in v3:
time: 146 us
  Pallas kernels  143 us (98%)
  local copies, waits for them, and re-layouts  1.64 us (1%)
    pallas_call x1, Pallas kernels, on_device(): pl.pallas_call(functools.partial(kernel, BATCHES), out_shape=jax.ShapeDty...  143 us

profile of v3, /device:TPU:1, one launch (start us, length us, event | category | flops | bytes accessed | tf_op | source)
XLA Modules:
  0.0 145.5 jit_solution(5654384152644792800)
XLA Ops:
  0.6 143.2 %shard_map.59 = bf16[2,12,16,256]{3,2,1,0:T(8,128)(2,1)} custom-call(bf16[1,2,256,2048]{3,2,1,0:T(8,128)(2,1)} %gd_ref.1, bf16[1,2,256,2048]{3,2,1,0:T(8,128)(2,1)} %gu_ref.1, bf16[1,2,96,256]{3,2,1,0:T(8,128)(2,1)} %sd_ref.1, bf16[1,2,96,256]{3,2,1,0:T(8,128)(2,1)} %su_ref.1), custom_call_target="tpu_custom_call" | custom-call | tf_op jit(solution)/shard_map/pallas_call | solution.py:373
  143.9 1.0 fusion
  144.8 0.7 copy_bitcast_fusion

commit v4 on v3

--- a/solution.py
+++ b/solution.py
@@ -23,6 +23,7 @@
     batches, gd_ref, gu_ref, sd_ref, su_ref, o_ref,
     graw, sraw, gt, src, ins, outs,
     g_sem, s_sem, gt_send, gt_recv, src_send, src_recv, send_sem, recv_sem, half_send, half_recv, o_sem,
+    swap_send, swap_recv, swap_src,
 ):
     shots = sd_ref.shape[2]
     width = shots // batches
@@ -38,8 +39,22 @@
     def worker_of(at, d):
         return jnp.where(((at == MID - 1) | (at == MID)) & (d == 0), 0, 1)
 
+    def flips(at, d):
+        plane = at // Y
+        return (d == 1) & ((plane == 1) | (plane == 3))
+
+    def host(at, d):
+        mirrored = at // Y * Y + Y - 1 - lax.rem(at, Y)
+        return jnp.where(flips(at, d), mirrored, at)
+
+    flipped = flips(layer, 1)
+    partner = host(layer, 1)
+
     def position(d):
-        return jnp.where(d == 0, layer, LAST - layer)
+        return jnp.where(d == 0, layer, LAST - partner)
+
+    def slot_of(d):
+        return jnp.where(flipped & (d == 1), 2, d)
 
     def load(d):
         def start(ref, at):
@@ -97,6 +112,21 @@
         half = src.at[d, :, :, pl.ds(c * ROWS, ROWS)]
         return remote(half, half, src_send.at[d], src_recv.at[d], sibling)
 
+    def swap_copy(c, p, q):
+        cols = pl.ds(p * PIECE + c * ROWS, ROWS)
+        a, z = gt.at[1, q, :, cols], gt.at[2, q, :, cols]
+        return remote(a, z, swap_send.at[p, q], swap_recv.at[c, p, q], (partner, 2 * y + 1))
+
+    def swap_source(c):
+        cols = pl.ds(c * ROWS, ROWS)
+        a, z = src.at[1, :, :, cols], src.at[2, :, :, cols]
+        return remote(a, z, swap_src.at[2], swap_src.at[c], (partner, 2 * y + 1))
+
+    def swap_out(b, c):
+        half = outs.at[1, b, :, pl.ds(c * ROWS, ROWS)]
+        sem = (half_send, o_sem)[c].at[1, b]
+        return remote(half, o_ref.at[1, b], sem, half_recv.at[1, b], (partner, 2 * y + c))
+
     def half_copy(d, b, c):
         half = outs.at[d, b, :, pl.ds((1 - c) * ROWS, ROWS)]
         return remote(half, o_ref.at[d, b], half_send.at[d, b], half_recv.at[d, b], sibling)
@@ -111,7 +141,7 @@
             pl.semaphore_signal(barrier, 1, device_id=(at, 2 * q + c), device_id_type=MESH)
 
     def targets(d):
-        at = jnp.where(d == 0, layer + 1, layer - 1)
+        at = jnp.where(d == 0, layer + 1, host(jnp.maximum(partner - 1, 0), 1))
         worker = worker_of(at, d)
         return [(at, 2 * lax.rem(y + off, Y) + worker) for off in range(Y)]
 
@@ -129,7 +159,7 @@
 
         for d in (first, second):
 
-            @pl.when(mine(d))
+            @pl.when(mine(d) & (slot_of(d) < 2))
             def _():
                 src_copy(d, 1 - c).wait_recv()
 
@@ -144,8 +174,18 @@
                     for kind in range(SENDS):
                         send(d, b, kind, targets(d)).wait_send()
 
-                half_copy(d, b, c).wait_send()
-                out_copy(d, b, c).wait()
+                if c == 1:
+
+                    @pl.when(slot_of(d) == 2)
+                    def _():
+                        for at in range(2):
+                            swap_out(b, at).wait_send()
+
+                @pl.when(slot_of(d) < 2)
+                def _():
+                    half_copy(d, b, c).wait_send()
+                    out_copy(d, b, c).wait()
+
                 return carry
 
             lax.fori_loop(0, batches, step, 0)
@@ -154,6 +194,7 @@
             d = jnp.where(k < batches, first, second)
             b = lax.rem(k, batches)
             pos = position(d)
+            slot = slot_of(d)
             to = targets(d)
 
             def send_all():
@@ -166,13 +207,30 @@
 
                     @pl.when(jnp.logical_not(central))
                     def _():
-                        transpose(second, c)
+                        def then(p, q):
+                            @pl.when(flipped)
+                            def _():
+                                swap_copy(c, p, q).start()
+
+                        transpose(second, c, then)
 
                     @pl.when(begin == 0)
                     def _():
                         drain(first)
 
-                for_gt(lambda copy: copy.wait_recv(), second, 1 - c)
+                if c == 1:
+
+                    @pl.when(flipped)
+                    def _():
+                        for at in range(2):
+                            swap_source(at).wait_recv()
+                            for p in range(2):
+                                for q in range(Y):
+                                    swap_copy(at, p, q).wait_recv()
+
+                @pl.when(slot_of(second) < 2)
+                def _():
+                    for_gt(lambda copy: copy.wait_recv(), second, 1 - c)
 
             @pl.when(pos == 0)
             def _():
@@ -187,7 +245,7 @@
                     rows = slice(t // 2 * SIDE, (t // 2 + 1) * SIDE)
                     for m in range(2):
                         at = (2 * m + t % 2) * SIDE
-                        pltpu.matmul_push_rhs(gt[d, q, rows, at : at + SIDE], t % 2, m)
+                        pltpu.matmul_push_rhs(gt[slot, q, rows, at : at + SIDE], t % 2, m)
 
                 def arrive(n, kind):
                     part = (d, b, order[n])
@@ -216,7 +274,7 @@
                     real = by_real[:width] - by_imag[width:]
                     imag = by_imag[:width] + by_real[width:]
                     cols = slice(h * SIDE, (h + 1) * SIDE)
-                    fresh = jnp.concatenate([real, imag], 0) + src[d, b, :, cols].astype(jnp.float32)
+                    fresh = jnp.concatenate([real, imag], 0) + src[slot, b, :, cols].astype(jnp.float32)
                     outs[d, b, :, cols] = fresh.astype(jnp.bfloat16)
 
             def compute():
@@ -232,8 +290,18 @@
             def _():
                 compute()
 
-            half_copy(d, b, c).start()
-            out_copy(d, b, c).start()
+            if c == 1:
+
+                @pl.when(slot == 2)
+                def _():
+                    for at in range(2):
+                        swap_out(b, at).start()
+
+            @pl.when(slot < 2)
+            def _():
+                half_copy(d, b, c).start()
+                out_copy(d, b, c).start()
+
             return carry
 
         lax.fori_loop(begin, end, step, 0)
@@ -241,7 +309,7 @@
 
     def serve(c):
         def helps(d):
-            return worker_of(layer, d) != c
+            return (worker_of(layer, d) != c) & (slot_of(d) < 2)
 
         def before():
             for d in (first, second):
@@ -249,6 +317,10 @@
                 @pl.when(helps(d))
                 def _():
                     src_copy(d, c).start()
+
+            @pl.when(flipped)
+            def _():
+                swap_source(c).start()
 
         def offer(d):
             def then(p, q):
@@ -256,6 +328,10 @@
                 def _():
                     gt_copy(d, c, p, q).start()
 
+                @pl.when(slot_of(d) == 2)
+                def _():
+                    swap_copy(c, p, q).start()
+
             transpose(d, c, then)
 
         def after():
@@ -274,6 +350,18 @@
                         for_gt(lambda copy: copy.wait_send(), d, c)
 
                     lax.fori_loop(0, batches, step, 0)
+
+            @pl.when(flipped)
+            def _():
+                def step(b, carry):
+                    swap_out(b, c).wait_recv()
+                    return carry
+
+                swap_source(c).wait_send()
+                for p in range(2):
+                    for q in range(Y):
+                        swap_copy(c, p, q).wait_send()
+                lax.fori_loop(0, batches, step, 0)
 
         return before, offer, after
 
@@ -295,9 +383,13 @@
             for hop in (-1, 1):
                 greet(layer + hop, worker_of(layer + hop, 0))
 
+        @pl.when(flipped)
+        def _():
+            pl.semaphore_signal(barrier, 1, device_id=(partner, 2 * y + 1), device_id_type=MESH)
+
         load(second)
         place_source(0)
-        pl.semaphore_wait(barrier, 1 + jnp.where(middle, 2 * Y, 0))
+        pl.semaphore_wait(barrier, 1 + jnp.where(middle, 2 * Y, 0) + jnp.where(flipped, 1, 0))
         before()
 
         @pl.when(position(first) > 0)
@@ -335,6 +427,19 @@
         @pl.when(near)
         def _():
             greet(jnp.where(layer < MID, MID - 1, MID), 0)
+
+        over = (layer == 3) | (layer == 4) | (layer == 11) | (layer == 12)
+        under = (layer == 7) | (layer == 8) | (layer == 15) | (layer == 16)
+        guests = guests + jnp.where(over | under, Y, 0) + jnp.where(flipped, 2, 0)
+
+        @pl.when(over | under)
+        def _():
+            greet(jnp.where(over, layer + Y, layer - Y), 1)
+
+        @pl.when(flipped)
+        def _():
+            for at in range(2):
+                pl.semaphore_signal(barrier, 1, device_id=(partner, 2 * y + at), device_id_type=MESH)
 
         load(second)
         place_source(1)
@@ -378,8 +483,8 @@
         scratch_shapes=[
             pltpu.VMEM((2, 2, ROWS, points), jnp.bfloat16),
             pltpu.VMEM((2, 2, shots, ROWS), jnp.bfloat16),
-            pltpu.VMEM((2, Y, PIECE, 2 * PIECE), jnp.bfloat16),
-            pltpu.VMEM((2, *trace), jnp.bfloat16),
+            pltpu.VMEM((3, Y, PIECE, 2 * PIECE), jnp.bfloat16),
+            pltpu.VMEM((3, *trace), jnp.bfloat16),
             pltpu.VMEM((2, BATCHES, Y, 2 * width, PIECE), jnp.bfloat16),
             pltpu.VMEM((2, *trace), jnp.bfloat16),
             dma((2, 2)),
@@ -393,6 +498,9 @@
             dma((2, BATCHES)),
             dma((2, BATCHES)),
             dma((2, BATCHES)),
+            dma((2, Y)),
+            dma((2, 2, Y)),
+            dma((3,)),
         ],
         compiler_params=pltpu.CompilerParams(
             collective_id=0, has_side_effects=True, vmem_limit_bytes=60 << 20

time: 146 us -> 143 us (0.979)
  Pallas kernels: 143 us -> 141 us
    pallas_call x1, Pallas kernels: 143 us -> 141 us  [on_device(): pl.pallas_call(functools.partial(kernel, BATCHES), out_shape=jax.ShapeDty...]
where the time goes in v4:
time: 143 us
  Pallas kernels  141 us (99%)
  local copies, waits for them, and re-layouts  1.64 us (1%)
    pallas_call x1, Pallas kernels, on_device(): pl.pallas_call(functools.partial(kernel, BATCHES), out_shape=jax.ShapeDty...  141 us

profile of v4, /device:TPU:1, one launch (start us, length us, event | category | flops | bytes accessed | tf_op | source)
XLA Modules:
  0.0 142.8 jit_solution(13508696802305182121)
XLA Ops:
  0.6 140.6 %shard_map.59 = bf16[2,12,16,256]{3,2,1,0:T(8,128)(2,1)} custom-call(bf16[1,2,256,2048]{3,2,1,0:T(8,128)(2,1)} %gd_ref.1, bf16[1,2,256,2048]{3,2,1,0:T(8,128)(2,1)} %gu_ref.1, bf16[1,2,96,256]{3,2,1,0:T(8,128)(2,1)} %sd_ref.1, bf16[1,2,96,256]{3,2,1,0:T(8,128)(2,1)} %su_ref.1), custom_call_target="tpu_custom_call" | custom-call | tf_op jit(solution)/shard_map/pallas_call | solution.py:478
  141.2 1.0 fusion
  142.1 0.7 copy_bitcast_fusion

commit v5 on v4

--- a/solution.py
+++ b/solution.py
@@ -72,13 +72,13 @@
     def load_wait(d, p):
         pltpu.make_async_copy(gd_ref.at[0, p], graw.at[d, p], g_sem.at[d, p]).wait()
 
-    def source_load(d):
-        ref = (sd_ref, su_ref)[d]
+    def source_load(which, d):
+        ref = (sd_ref, su_ref)[which]
         return pltpu.make_async_copy(ref.at[0], sraw.at[d], s_sem.at[d])
 
-    def place_source(c):
-        for d in range(2):
-            source_load(d).wait()
+    def place_source(c, *sweeps):
+        for d in sweeps:
+            source_load(0, d).wait()
             for b in range(batches):
                 rows = [sraw[d, p, b * width : (b + 1) * width, :].astype(jnp.float32) for p in range(2)]
                 src[d, b, :, c * ROWS : (c + 1) * ROWS] = jnp.concatenate(rows, 0).astype(jnp.bfloat16)
@@ -122,17 +122,21 @@
         a, z = src.at[1, :, :, cols], src.at[2, :, :, cols]
         return remote(a, z, swap_src.at[2], swap_src.at[c], (partner, 2 * y + 1))
 
-    def swap_out(b, c):
-        half = outs.at[1, b, :, pl.ds(c * ROWS, ROWS)]
-        sem = (half_send, o_sem)[c].at[1, b]
-        return remote(half, o_ref.at[1, b], sem, half_recv.at[1, b], (partner, 2 * y + c))
-
-    def half_copy(d, b, c):
-        half = outs.at[d, b, :, pl.ds((1 - c) * ROWS, ROWS)]
-        return remote(half, o_ref.at[d, b], half_send.at[d, b], half_recv.at[d, b], sibling)
-
-    def out_copy(d, b, c):
-        return pltpu.make_async_copy(outs.at[d, b, :, pl.ds(c * ROWS, ROWS)], o_ref.at[d, b], o_sem.at[d, b])
+    def pair(j):
+        return pl.ds(2 * j, 2)
+
+    def swap_out(j, c):
+        half = outs.at[1, pair(j), :, pl.ds(c * ROWS, ROWS)]
+        sem = (half_send, o_sem)[c].at[1, j]
+        return remote(half, o_ref.at[1, pair(j)], sem, half_recv.at[1, j], (partner, 2 * y + c))
+
+    def half_copy(d, j, c):
+        half = outs.at[d, pair(j), :, pl.ds((1 - c) * ROWS, ROWS)]
+        return remote(half, o_ref.at[d, pair(j)], half_send.at[d, j], half_recv.at[d, j], sibling)
+
+    def out_copy(d, j, c):
+        half = outs.at[d, pair(j), :, pl.ds(c * ROWS, ROWS)]
+        return pltpu.make_async_copy(half, o_ref.at[d, pair(j)], o_sem.at[d, j])
 
     barrier = pltpu.get_barrier_semaphore()
 
@@ -157,11 +161,9 @@
         def mine(d):
             return worker_of(layer, d) == c
 
-        for d in (first, second):
-
-            @pl.when(mine(d) & (slot_of(d) < 2))
-            def _():
-                src_copy(d, 1 - c).wait_recv()
+        @pl.when(mine(first))
+        def _():
+            src_copy(first, 1 - c).wait_recv()
 
         @pl.when(mine(first) & (position(first) > 0))
         def _():
@@ -174,21 +176,25 @@
                     for kind in range(SENDS):
                         send(d, b, kind, targets(d)).wait_send()
 
+                return carry
+
+            def written(j, carry):
                 if c == 1:
 
                     @pl.when(slot_of(d) == 2)
                     def _():
                         for at in range(2):
-                            swap_out(b, at).wait_send()
+                            swap_out(j, at).wait_send()
 
                 @pl.when(slot_of(d) < 2)
                 def _():
-                    half_copy(d, b, c).wait_send()
-                    out_copy(d, b, c).wait()
+                    half_copy(d, j, c).wait_send()
+                    out_copy(d, j, c).wait()
 
                 return carry
 
             lax.fori_loop(0, batches, step, 0)
+            lax.fori_loop(0, batches // 2, written, 0)
 
         def step(k, carry):
             d = jnp.where(k < batches, first, second)
@@ -230,6 +236,7 @@
 
                 @pl.when(slot_of(second) < 2)
                 def _():
+                    src_copy(second, 1 - c).wait_recv()
                     for_gt(lambda copy: copy.wait_recv(), second, 1 - c)
 
             @pl.when(pos == 0)
@@ -290,17 +297,18 @@
             def _():
                 compute()
 
+            both, j = lax.rem(b, 2) == 1, b // 2
             if c == 1:
 
-                @pl.when(slot == 2)
+                @pl.when(both & (slot == 2))
                 def _():
                     for at in range(2):
-                        swap_out(b, at).start()
-
-            @pl.when(slot < 2)
-            def _():
-                half_copy(d, b, c).start()
-                out_copy(d, b, c).start()
+                        swap_out(j, at).start()
+
+            @pl.when(both & (slot < 2))
+            def _():
+                half_copy(d, j, c).start()
+                out_copy(d, j, c).start()
 
             return carry
 
@@ -312,11 +320,15 @@
             return (worker_of(layer, d) != c) & (slot_of(d) < 2)
 
         def before():
-            for d in (first, second):
-
-                @pl.when(helps(d))
-                def _():
-                    src_copy(d, c).start()
+            @pl.when(helps(first))
+            def _():
+                src_copy(first, c).start()
+
+            place_source(c, second)
+
+            @pl.when(helps(second))
+            def _():
+                src_copy(second, c).start()
 
             @pl.when(flipped)
             def _():
@@ -339,8 +351,8 @@
 
                 @pl.when(helps(d))
                 def _():
-                    def step(b, carry):
-                        half_copy(d, b, 1 - c).wait_recv()
+                    def step(j, carry):
+                        half_copy(d, j, 1 - c).wait_recv()
                         return carry
 
                     src_copy(d, c).wait_send()
@@ -349,24 +361,24 @@
                     def _():
                         for_gt(lambda copy: copy.wait_send(), d, c)
 
-                    lax.fori_loop(0, batches, step, 0)
+                    lax.fori_loop(0, batches // 2, step, 0)
 
             @pl.when(flipped)
             def _():
-                def step(b, carry):
-                    swap_out(b, c).wait_recv()
+                def step(j, carry):
+                    swap_out(j, c).wait_recv()
                     return carry
 
                 swap_source(c).wait_send()
                 for p in range(2):
                     for q in range(Y):
                         swap_copy(c, p, q).wait_send()
-                lax.fori_loop(0, batches, step, 0)
+                lax.fori_loop(0, batches // 2, step, 0)
 
         return before, offer, after
 
     for d in range(2):
-        source_load(d).start()
+        source_load(d, d).start()
     load(first)
     pl.semaphore_signal(barrier, 1, device_id=sibling, device_id_type=MESH)
 
@@ -388,7 +400,7 @@
             pl.semaphore_signal(barrier, 1, device_id=(partner, 2 * y + 1), device_id_type=MESH)
 
         load(second)
-        place_source(0)
+        place_source(0, first)
         pl.semaphore_wait(barrier, 1 + jnp.where(middle, 2 * Y, 0) + jnp.where(flipped, 1, 0))
         before()
 
@@ -442,7 +454,7 @@
                 pl.semaphore_signal(barrier, 1, device_id=(partner, 2 * y + at), device_id_type=MESH)
 
         load(second)
-        place_source(1)
+        place_source(1, first)
 
         @pl.when((position(first) > 0) & jnp.logical_not(middle))
         def _():
@@ -495,9 +507,9 @@
             dma((2,)),
             dma((2, BATCHES, SENDS)),
             dma((2, BATCHES, SENDS)),
-            dma((2, BATCHES)),
-            dma((2, BATCHES)),
-            dma((2, BATCHES)),
+            dma((2, BATCHES // 2)),
+            dma((2, BATCHES // 2)),
+            dma((2, BATCHES // 2)),
             dma((2, Y)),
             dma((2, 2, Y)),
             dma((3,)),

time: 143 us -> 143 us (level)
  no operation moved by 1% of the time
where the time goes in v5:
time: 143 us; the launch traced here: 142 us
  Pallas kernels  140 us (98%)
  local copies, waits for them, and re-layouts  1.64 us (1%)
    pallas_call x1, Pallas kernels, on_device(): pl.pallas_call(functools.partial(kernel, BATCHES), out_shape=jax.ShapeDty...  140 us

profile of v5, /device:TPU:1, one launch (start us, length us, event | category | flops | bytes accessed | tf_op | source)
XLA Modules:
  0.0 142.5 jit_solution(3288367380805123032)
XLA Ops:
  0.6 140.2 %shard_map.59 = bf16[2,12,16,256]{3,2,1,0:T(8,128)(2,1)} custom-call(bf16[1,2,256,2048]{3,2,1,0:T(8,128)(2,1)} %gd_ref.1, bf16[1,2,256,2048]{3,2,1,0:T(8,128)(2,1)} %gu_ref.1, bf16[1,2,96,256]{3,2,1,0:T(8,128)(2,1)} %sd_ref.1, bf16[1,2,96,256]{3,2,1,0:T(8,128)(2,1)} %su_ref.1), custom_call_target="tpu_custom_call" | custom-call | tf_op jit(solution)/shard_map/pallas_call | solution.py:490
  140.8 1.0 fusion
  141.8 0.7 copy_bitcast_fusion

commit v6 on v5

--- a/solution.py
+++ b/solution.py
@@ -79,9 +79,12 @@
     def place_source(c, *sweeps):
         for d in sweeps:
             source_load(0, d).wait()
-            for b in range(batches):
-                rows = [sraw[d, p, b * width : (b + 1) * width, :].astype(jnp.float32) for p in range(2)]
-                src[d, b, :, c * ROWS : (c + 1) * ROWS] = jnp.concatenate(rows, 0).astype(jnp.bfloat16)
+            for j in range(batches // 2):
+                both = [sraw[d, p, 2 * j * width : 2 * (j + 1) * width, :].astype(jnp.float32) for p in range(2)]
+                for h in range(2):
+                    rows = [part[h * width : (h + 1) * width] for part in both]
+                    placed = jnp.concatenate(rows, 0).astype(jnp.bfloat16)
+                    src[d, 2 * j + h, :, c * ROWS : (c + 1) * ROWS] = placed
 
     def transpose(d, c, then=None):
         for p in range(2):

time: 143 us -> 143 us (level)
  no operation moved by 1% of the time
where the time goes in v6:
time: 143 us; the launch traced here: 142 us
  Pallas kernels  140 us (98%)
  local copies, waits for them, and re-layouts  1.64 us (1%)
    pallas_call x1, Pallas kernels, on_device(): pl.pallas_call(functools.partial(kernel, BATCHES), out_shape=jax.ShapeDty...  140 us

profile of v6, /device:TPU:1, one launch (start us, length us, event | category | flops | bytes accessed | tf_op | source)
XLA Modules:
  0.0 142.5 jit_solution(3288367380805123032)
XLA Ops:
  0.6 140.2 %shard_map.59 = bf16[2,12,16,256]{3,2,1,0:T(8,128)(2,1)} custom-call(bf16[1,2,256,2048]{3,2,1,0:T(8,128)(2,1)} %gd_ref.1, bf16[1,2,256,2048]{3,2,1,0:T(8,128)(2,1)} %gu_ref.1, bf16[1,2,96,256]{3,2,1,0:T(8,128)(2,1)} %sd_ref.1, bf16[1,2,96,256]{3,2,1,0:T(8,128)(2,1)} %su_ref.1), custom_call_target="tpu_custom_call" | custom-call | tf_op jit(solution)/shard_map/pallas_call | solution.py:493
  140.8 1.0 fusion
  141.8 0.7 copy_bitcast_fusion
